TPU v7x, 32 devices: a whole 2x2x4 slice. The times are simulated.
32 devices in a mesh: parts: 2 (over y), row: 8 (over z, x), col: 2 (over core).
Axes of the slice: x: 2, y: 2, z: 4, core: 2. Of those that a mesh axis runs over, the one named last changes fastest.
Arguments:
- features: bfloat16 [24576, 128], P(('parts', 'row', 'col')), parts along dimension 0, may hold values from -12 to 12
- labels: int32 [24576], P(('parts', 'row', 'col')), parts along dimension 0, may hold values from 0 to 171
- train_mask: int32 [24576], P(('parts', 'row', 'col')), parts along dimension 0, may hold values from 0 to 1, as said below
- w_one: bfloat16 [128, 256], replicated, may hold values from -0.5 to 0.5
- w_two: bfloat16 [256, 172], replicated, may hold values from -1 to 3.5
- tile_rows: int32 [16, 2, 70], P(('parts', 'row'), 'col'), parts along dimension 0, may hold values from 0 to 11, as said below
- tile_cols: int32 [16, 2, 70], P(('parts', 'row'), 'col'), parts along dimension 0, may hold values from 0 to 47, as said below
- tile_count: int32 [16, 2], P(('parts', 'row'), 'col'), parts along dimension 0, may hold values from 22 to 70, as said below
- edge_dst: int32 [16, 2, 70, 128], P(('parts', 'row'), 'col'), parts along dimension 0, may hold values from 0 to 127
- edge_src: int32 [16, 2, 70, 128], P(('parts', 'row'), 'col'), parts along dimension 0, may hold values from 0 to 127
Outputs:
- logits: float32 [24576, 172], P(('parts', 'row', 'col')), parts along dimension 0
- loss: float32 [2], P('parts'), parts along dimension 0
- grad_one: float32 [256, 256], P('parts'), parts along dimension 0
- grad_two: float32 [512, 172], P('parts'), parts along dimension 0
There are 2 independent parts, one for each index of `parts`. A program takes and returns all parts, laid end to end along the dimension named above; an argument that names none is the same for every part. Nothing has to cross between parts.
Inputs may be any that keep to these rules, and one draw needn't show every extreme that they name: `tile_rows`: which tile of the device's block row, 12 tiles of two node blocks, a slot's destination nodes lie in. Live slots of one device name distinct tiles, listed first. The source tile of a live slot of grid row r is owned by grid row r, r + 1, r - 1, r + 2 or r - 8 / 4 (modulo 8), namely row tile_cols div 6. `tile_count`: A is symmetric. Some device fills all 70 slots. `train_mask`: the first node of every tile is a training node.
All inputs are finite; a program needn't handle non-finite values.
Results may differ from a plain program's by a relative error of at most 0.0085.
The roundings to bfloat16 on the way count: a program that leaves them out, or rounds other values in their place, can miss the bound.
Values sent between devices are 32-bit elements; how exact they have to be, the bound alone decides.
A program may use at most 64 MiB of HBM per device.

v0:
```python
import jax
import jax.numpy as jnp
from jax import lax
from jax.sharding import PartitionSpec as P

TILE = 128


def from_behind(value, axis, by):
    peers = lax.axis_size(axis)
    return lax.ppermute(value, axis, [(i, (i + by) % peers) for i in range(peers)])


def shards(
    features, labels, train_mask, w_one, w_two, tile_rows, tile_cols, tile_count, edge_dst, edge_src
):
    block_rows = features.shape[0]
    owned_tiles = block_rows // TILE
    row_total = lax.axis_size("row")
    quarter = row_total // 4
    here_row = lax.axis_index("row")
    classes_total = w_two.shape[1]
    lane_ids = lax.iota(jnp.int32, TILE)
    offsets = [0, 1, -1, quarter, -quarter]
    slot_rows = tile_rows[0, 0]
    slot_cols = tile_cols[0, 0]
    slot_total = slot_rows.shape[0]
    live_slot = (lax.iota(jnp.int32, slot_total) < tile_count[0, 0]).astype(jnp.bfloat16)
    dst_onehot = (edge_dst[0, 0][:, :, None] == lane_ids).astype(jnp.bfloat16) * live_slot[
        :, None, None
    ]
    src_onehot = (edge_src[0, 0][:, :, None] == lane_ids).astype(jnp.bfloat16)
    dense_tiles = jnp.einsum(
        "teu,tev->tuv", dst_onehot, src_onehot, preferred_element_type=jnp.float32
    ).astype(jnp.bfloat16)
    row_select = (slot_rows[:, None] == lax.iota(jnp.int32, 2 * owned_tiles)[None, :]).astype(
        jnp.bfloat16
    )
    distance = (slot_cols // owned_tiles - here_row) % row_total
    position = sum(
        (
            index_value * (distance == offset_value % row_total).astype(jnp.int32)
            for index_value, offset_value in enumerate(offsets)
        )
    )
    prepare_slot_index = 0 + position * owned_tiles + slot_cols % owned_tiles
    dense_tiles, row_select, slot_index = (dense_tiles, row_select, prepare_slot_index)
    row_weights = row_select.astype(jnp.float32)
    tiles_wide = dense_tiles.astype(jnp.float32)

    def fetch(node_block):
        node_block = node_block.astype(jnp.float32)
        pieces = [node_block] + [from_behind(node_block, "row", -shift_by) for shift_by in (1, -1)]
        pieces = pieces + [
            from_behind(node_block, "row", -shift_by) for shift_by in (quarter, -quarter)
        ]
        buffer_rows = jnp.concatenate(pieces, axis=0)
        return buffer_rows

    def spread(node_block):
        col_width = node_block.shape[1]
        buffer_rows = fetch(node_block).reshape(-1, TILE, col_width)
        picked = jnp.take(buffer_rows, slot_index, axis=0)
        product = jnp.einsum(
            "tuv,tvw->tuw",
            tiles_wide,
            picked,
            preferred_element_type=jnp.float32,
            precision=lax.Precision.HIGHEST,
        )
        return jnp.einsum(
            "ta,tuw->auw", row_weights, product, precision=lax.Precision.HIGHEST
        ).reshape(2 * owned_tiles * TILE, col_width)

    train_f = train_mask.astype(jnp.float32)
    degree_part = jnp.einsum(
        "ta,tuv->au", row_select, dense_tiles, preferred_element_type=jnp.float32
    ).reshape(-1)
    first_terms = spread(features)
    first_sum, degree_sum = (
        lax.psum_scatter(first_terms, "col", scatter_dimension=0, tiled=True),
        lax.psum_scatter(degree_part, "col", scatter_dimension=0, tiled=True),
    )
    degree = 1.0 + degree_sum
    agg_one = ((first_sum + features.astype(jnp.float32)) / degree[:, None]).astype(jnp.bfloat16)
    hidden = jnp.maximum(jnp.dot(agg_one, w_one, preferred_element_type=jnp.float32), 0.0).astype(
        jnp.bfloat16
    )
    projected = jnp.dot(hidden, w_two, preferred_element_type=jnp.float32)
    logit_terms = spread(projected)
    logit_sum = lax.psum_scatter(logit_terms, "col", scatter_dimension=0, tiled=True)
    logits = (logit_sum + projected) / degree[:, None]
    row_max = jnp.max(logits, axis=1, keepdims=True)
    log_total = row_max[:, 0] + jnp.log(jnp.sum(jnp.exp(logits - row_max), axis=1))
    onehot = (labels[:, None] == lax.iota(jnp.int32, classes_total)[None, :]).astype(jnp.float32)
    picked_logit = jnp.sum(onehot * logits, axis=1)
    loss_local = jnp.sum(train_f * (log_total - picked_logit))
    loss_total, train_count = lax.psum((loss_local, jnp.sum(train_f)), ("row", "col"))
    probabilities = jnp.exp(logits - log_total[:, None])
    logit_grad = train_f[:, None] * (probabilities - onehot) / train_count
    error_scaled = (logit_grad / degree[:, None]).astype(jnp.bfloat16)
    error_terms = spread(error_scaled)
    back_sum = lax.psum_scatter(error_terms, "col", scatter_dimension=0, tiled=True)
    proj_grad = (back_sum + error_scaled.astype(jnp.float32)).astype(jnp.bfloat16)
    grad_two = lax.dot_general(
        hidden, proj_grad, (((0,), (0,)), ((), ())), preferred_element_type=jnp.float32
    )
    grad_two = lax.psum(grad_two, ("row", "col"))
    hidden_grad = lax.dot_general(
        proj_grad, w_two, (((1,), (1,)), ((), ())), preferred_element_type=jnp.float32
    )
    active_grad = jnp.where(hidden > 0, hidden_grad, 0.0).astype(jnp.bfloat16)
    grad_one = lax.dot_general(
        agg_one, active_grad, (((0,), (0,)), ((), ())), preferred_element_type=jnp.float32
    )
    grad_one = lax.psum(grad_one, ("row", "col"))
    return (logits, (loss_total / train_count).reshape(1), grad_one, grad_two)


def solution(mesh):
    return jax.shard_map(
        shards,
        mesh=mesh,
        in_specs=(
            P(("parts", "row", "col"), None),
            P(("parts", "row", "col")),
            P(("parts", "row", "col")),
            P(),
            P(),
            P(("parts", "row"), "col", None),
            P(("parts", "row"), "col", None),
            P(("parts", "row"), "col"),
            P(("parts", "row"), "col", None, None),
            P(("parts", "row"), "col", None, None),
        ),
        out_specs=(
            P(("parts", "row", "col"), None),
            P("parts"),
            P("parts", None),
            P("parts", None),
        ),
        check_vma=False,
    )
```

profile of v0, /device:TPU:0, one launch (start us, length us, event | category | flops | bytes accessed | tf_op | source)
XLA Modules:
  0.0 350.3 jit_solution(11017643264689319075)
XLA Ops:
  8.2 3.1 collective-permute-start.3
  11.3 2.1 collective-permute-start.2
  15.0 3.1 collective-permute-start
  21.2 2.9 convert_reduce_fusion
  24.8 11.7 %collective-permute-done = f32[768,128]{1,0:T(8,128)} collective-permute-done((f32[768,128]{1,0:T(8,128)S(1)}, f32[768,128]{1,0:T(8,128)}, u32[]{:S(2)}, u32[]{:S(2)}) %collective-permute-start) | collective-permute-done | bytes 393248 | tf_op jit(solution)/shard_map/ppermute | solution.py:11
  44.7 4.5 %gather_fusion = f32[70,128,128]{2,1,0:T(8,128)} fusion(f32[30,128,128]{2,1,0:T(8,128)} %bitcast.6, s32[1024]{0:T(1024)S(1)} %pad_clamp_fusion.1), kind=kCustom, calls=%fused_computation.2 | custom fusion | bytes 9175320 | tf_op jit(solution)/shard_map/jit(_take)/gather | solution.py:63
  49.2 5.3 %fusion.10 = f32[70,128,128]{2,1,0:T(8,128)S(1)} fusion(bf16[70,128,128]{1,2,0:T(8,128)(2,1)S(1)} %get-tuple-element.21, f32[70,128,128]{2,1,0:T(8,128)} %gather_fusion, pred[70]{0:T(512)(128)(4,1)S(1)} %get-tuple-element.18), kind=kOutput, calls=%fused_computation.14 | convolution fusion | flops 1762754560 | bytes 11468870 | tf_op jit(solution)/shard_map/tuv,tvw->tuw/dot_general | solution.py:64
  54.5 4.2 %fusion.8 = f32[12,128,128]{2,0,1:T(8,128)S(1)} fusion(f32[70,128,128]{2,1,0:T(8,128)S(1)} %fusion.10, s32[70]{0:T(128)S(1)} %bitcast.91), kind=kOutput, calls=%fused_computation.11 | convolution fusion | flops 165151552 | bytes 5374232 | tf_op jit(solution)/shard_map/ta,tuw->auw/dot_general | solution.py:71
  61.4 2.5 all-reduce
  63.9 4.6 %reduce-scatter.4.cloned.1.call-done = f32[768,128]{1,0:T(8,128)} async-done(((f32[1536,128]{1,0:T(8,128)}), f32[768,128]{1,0:T(8,128)}) %reduce-scatter.4.cloned.1.call-update) | async-done | bytes 393232 | tf_op jit(solution)/shard_map/reduce_scatter | solution.py:81
  70.3 4.5 %collective-permute-start.4 = (f32[768,172]{0,1:T(8,128)S(1)}, f32[768,172]{0,1:T(8,128)S(1)}, u32[]{:S(2)}, u32[]{:S(2)}) collective-permute-start(f32[768,172]{0,1:T(8,128)S(1)} %get-tuple-element.23), channel_id=1, source_target_pairs={{0,14},{2,0},{4,2},{6,4},{8,6},{10,8},{12,10},{14,12},{1,15},{3,1}... | collective-permute-start | bytes 1585160 | tf_op jit(solution)/shard_map/ppermute | solution.py:11
  77.5 18.9 %collective-permute-done.4 = f32[768,172]{0,1:T(8,128)S(1)} collective-permute-done((f32[768,172]{0,1:T(8,128)S(1)}, f32[768,172]{0,1:T(8,128)S(1)}, u32[]{:S(2)}, u32[]{:S(2)}) %collective-permute-start.4) | collective-permute-done | bytes 528416 | tf_op jit(solution)/shard_map/ppermute | solution.py:11
  96.6 2.4 collective-permute-done.6
  99.1 11.9 %collective-permute-done.7 = f32[768,172]{0,1:T(8,128)S(1)} collective-permute-done((f32[768,172]{0,1:T(8,128)S(1)}, f32[768,172]{0,1:T(8,128)S(1)}, u32[]{:S(2)}, u32[]{:S(2)}) %collective-permute-start.7) | collective-permute-done | bytes 528416 | tf_op jit(solution)/shard_map/ppermute | solution.py:11
  111.0 2.3 reshape.217
  113.3 3.3 copy.20
  116.6 3.6 %gather_fusion.1 = f32[70,128,172]{1,2,0:T(8,128)} fusion(f32[30,128,172]{1,2,0:T(8,128)S(1)} %copy.20, s32[1024]{0:T(1024)S(1)} %pad_clamp_fusion), kind=kCustom, calls=%fused_computation.clone | custom fusion | bytes 12329240 | tf_op jit(solution)/shard_map/jit(_take)/gather | solution.py:63
  120.3 6.0 %fusion.6 = f32[70,128,172]{1,2,0:T(8,128)S(1)} fusion(bf16[70,128,128]{1,2,0:T(8,128)(2,1)} %copy-done.1, f32[70,128,172]{1,2,0:T(8,128)} %gather_fusion.1, pred[70]{0:T(512)(128)(4,1)S(1)} %get-tuple-element.18), kind=kOutput, calls=%fused_computation.9 | convolution fusion | flops 2368701440 | bytes 14622790 | tf_op jit(solution)/shard_map/tuv,tvw->tuw/dot_general | solution.py:64
  126.2 3.8 %fusion.26 = f32[172,12,128]{2,1,0:T(8,128)S(1)} fusion(f32[70,128,172]{1,2,0:T(8,128)S(1)} %fusion.6, s32[70]{0:T(128)S(1)} %bitcast.93), kind=kOutput, calls=%fused_computation.29 | convolution fusion | flops 221922112 | bytes 7221528 | tf_op jit(solution)/shard_map/ta,tuw->auw/dot_general | solution.py:71
  131.7 9.8 %reduce-scatter.6.cloned.1.call-done = f32[768,172]{0,1:T(8,128)} async-done(((f32[1536,172]{0,1:T(8,128)}), f32[768,172]{0,1:T(8,128)}) %reduce-scatter.6.cloned.1.call-update) | async-done | bytes 528400 | tf_op jit(solution)/shard_map/reduce_scatter | solution.py:91
  143.4 34.6 %all-reduce.1 = (f32[]{:T(128)}, f32[]{:T(128)}) all-reduce(f32[]{:T(128)} %get-tuple-element.8, f32[]{:T(128)} %get-tuple-element.7), channel_id=1, replica_groups=mesh['parts'=2,'row'=8,'col'=2] {'row','col'}, use_global_device_ids=true, to_apply=%region_8.10 | all-reduce | flops 2 | bytes 16 | tf_op jit(solution)/shard_map/psum | solution.py:98
  181.0 2.0 collective-permute-start.11
  183.0 17.3 %collective-permute-done.8 = f32[768,172]{0,1:T(8,128)S(1)} collective-permute-done((f32[768,172]{0,1:T(8,128)S(1)}, f32[768,172]{0,1:T(8,128)S(1)}, u32[]{:S(2)}, u32[]{:S(2)}) %collective-permute-start.8) | collective-permute-done | bytes 528416 | tf_op jit(solution)/shard_map/ppermute | solution.py:11
  200.4 2.9 collective-permute-done.10
  203.3 10.3 %collective-permute-done.11 = f32[768,172]{0,1:T(8,128)S(1)} collective-permute-done((f32[768,172]{0,1:T(8,128)S(1)}, f32[768,172]{0,1:T(8,128)S(1)}, u32[]{:S(2)}, u32[]{:S(2)}) %collective-permute-start.11) | collective-permute-done | bytes 528416 | tf_op jit(solution)/shard_map/ppermute | solution.py:11
  213.7 2.2 reshape.220
  215.9 3.3 copy.23
  219.2 3.8 %gather_fusion.2 = f32[70,128,172]{1,2,0:T(8,128)} fusion(f32[30,128,172]{1,2,0:T(8,128)S(1)} %copy.23, s32[1024]{0:T(1024)} %copy-done.17), kind=kCustom, calls=%fused_computation.1.clone | custom fusion | bytes 12329240 | tf_op jit(solution)/shard_map/jit(_take)/gather | solution.py:63
  223.0 6.0 %fusion.4 = f32[70,128,172]{1,2,0:T(8,128)S(1)} fusion(bf16[70,128,128]{1,2,0:T(8,128)(2,1)} %copy-done.1, f32[70,128,172]{1,2,0:T(8,128)} %gather_fusion.2, pred[70]{0:T(512)(128)(4,1)S(1)} %copy-done.16), kind=kOutput, calls=%fused_computation.7 | convolution fusion | flops 2368701440 | bytes 14622790 | tf_op jit(solution)/shard_map/tuv,tvw->tuw/dot_general | solution.py:64
  229.0 3.8 %fusion.29 = f32[172,12,128]{2,1,0:T(8,128)S(1)} fusion(f32[70,128,172]{1,2,0:T(8,128)S(1)} %fusion.4, s32[70]{0:T(128)S(1)} %bitcast.94), kind=kOutput, calls=%fused_computation.30 | convolution fusion | flops 221922112 | bytes 7221528 | tf_op jit(solution)/shard_map/ta,tuw->auw/dot_general | solution.py:71
  234.4 10.9 %reduce-scatter.8.cloned.1.call-done = f32[768,172]{0,1:T(8,128)} async-done(((f32[1536,172]{0,1:T(8,128)}), f32[768,172]{0,1:T(8,128)}) %reduce-scatter.8.cloned.1.call-update) | async-done | bytes 528400 | tf_op jit(solution)/shard_map/reduce_scatter | solution.py:103
  249.8 89.6 %all-reduce.5.cloned.1.call-done = (f32[128,256]{1,0:T(8,128)}, f32[256,172]{0,1:T(8,128)}) async-done(((f32[128,256]{1,0:T(8,128)}, f32[256,172]{0,1:T(8,128)}), (f32[128,256]{1,0:T(8,128)}, f32[256,172]{0,1:T(8,128)})) %all-reduce.5.cloned.1.call-update) | async-done | bytes 307216 | tf_op jit(solution)/shard_map/psum | solution.py:116
  (102 shorter events, 35.2 us)
Async XLA Ops:
  7.2 62.8 %copy-start = (bf16[256,172]{0,1:T(8,128)(2,1)S(1)}, bf16[256,172]{0,1:T(8,128)(2,1)}, u32[]{:S(2)}) copy-start(bf16[256,172]{0,1:T(8,128)(2,1)} %param.16) | copy-start | bytes 264196
  7.2 61.3 %reduce-scatter.4.cloned.1.call-start = ((), (), s32[]{:S(2)}) async-start(), calls=%async_computation.3 | async-start | bytes 1179648 | tf_op jit(solution)/shard_map/reduce_scatter | solution.py:81
  8.2 35.7 %collective-permute-start.3 = (f32[768,128]{1,0:T(8,128)S(1)}, f32[768,128]{1,0:T(8,128)S(1)}, u32[]{:S(2)}, u32[]{:S(2)}) collective-permute-start(f32[768,128]{1,0:T(8,128)S(1)} %convert_element_type.67), channel_id=1, source_target_pairs={{0,4},{2,6},{4,8},{6,10},{8,12},{10,14},{12,0},{14,2},{1,5},{3,7},... | collective-permute-start | bytes 1179656 | tf_op jit(solution)/shard_map/ppermute | solution.py:11
  11.3 30.9 %collective-permute-start.2 = (f32[768,128]{1,0:T(8,128)S(1)}, f32[768,128]{1,0:T(8,128)}, u32[]{:S(2)}, u32[]{:S(2)}) collective-permute-start(f32[768,128]{1,0:T(8,128)S(1)} %convert_element_type.67), channel_id=1, source_target_pairs={{0,12},{2,14},{4,0},{6,2},{8,4},{10,6},{12,8},{14,10},{1,13},{3,15... | collective-permute-start | bytes 1179656 | tf_op jit(solution)/shard_map/ppermute | solution.py:11
  13.4 27.0 %collective-permute-start.1 = (f32[768,128]{1,0:T(8,128)S(1)}, f32[768,128]{1,0:T(8,128)}, u32[]{:S(2)}, u32[]{:S(2)}) collective-permute-start(f32[768,128]{1,0:T(8,128)S(1)} %convert_element_type.67), channel_id=1, source_target_pairs={{0,2},{2,4},{4,6},{6,8},{8,10},{10,12},{12,14},{14,0},{1,3},{3,5},... | collective-permute-start | bytes 1179656 | tf_op jit(solution)/shard_map/ppermute | solution.py:11
  15.0 21.5 %collective-permute-start = (f32[768,128]{1,0:T(8,128)S(1)}, f32[768,128]{1,0:T(8,128)}, u32[]{:S(2)}, u32[]{:S(2)}) collective-permute-start(f32[768,128]{1,0:T(8,128)S(1)} %convert_element_type.67), channel_id=1, source_target_pairs={{0,14},{2,0},{4,2},{6,4},{8,6},{10,8},{12,10},{14,12},{1,15},{3,1}... | collective-permute-start | bytes 1179656 | tf_op jit(solution)/shard_map/ppermute | solution.py:11
  24.2 25.0 %copy-start.1 = (bf16[70,128,128]{1,2,0:T(8,128)(2,1)}, bf16[70,128,128]{1,2,0:T(8,128)(2,1)S(1)}, u32[]{:S(2)}) copy-start(bf16[70,128,128]{1,2,0:T(8,128)(2,1)S(1)} %get-tuple-element.21) | copy-start | bytes 6881284
  24.8 95.5 %copy-start.15 = (pred[70]{0:T(512)(128)(4,1)}, pred[70]{0:T(512)(128)(4,1)S(1)}, u32[]{:S(2)}) copy-start(pred[70]{0:T(512)(128)(4,1)S(1)} %get-tuple-element.18) | copy-start | bytes 214
  54.5 5.5 %copy-start.19 = (u32[32]{0:T(128)S(1)}, u32[32]{0:T(128)}, u32[]{:S(2)}) copy-start(u32[32]{0:T(128)} %constant.94) | copy-start | bytes 388
  58.8 9.7 %copy-start.9 = (bf16[768,128]{1,0:T(8,128)(2,1)S(1)}, bf16[768,128]{1,0:T(8,128)(2,1)}, u32[]{:S(2)}) copy-start(bf16[768,128]{1,0:T(8,128)(2,1)} %param.12) | copy-start | bytes 589828
  58.8 10.9 %copy-start.10 = (bf16[128,256]{1,0:T(8,128)(2,1)S(1)}, bf16[128,256]{1,0:T(8,128)(2,1)}, u32[]{:S(2)}) copy-start(bf16[128,256]{1,0:T(8,128)(2,1)} %param.15) | copy-start | bytes 196612
  59.9 81.5 %reduce-scatter.6.cloned.1.call-start = ((), (), s32[]{:S(2)}) async-start(), calls=%async_computation.4 | async-start | bytes 1622016 | tf_op jit(solution)/shard_map/reduce_scatter | solution.py:91
  69.9 29.1 %copy-start.3 = (bf16[768,256]{1,0:T(8,128)(2,1)}, bf16[768,256]{1,0:T(8,128)(2,1)S(1)}, u32[]{:S(2)}) copy-start(bf16[768,256]{1,0:T(8,128)(2,1)S(1)} %fusion.32) | copy-start | bytes 1179652
  70.2 40.8 %copy-start.5 = (f32[768,172]{0,1:T(8,128)}, f32[768,172]{0,1:T(8,128)S(1)}, u32[]{:S(2)}) copy-start(f32[768,172]{0,1:T(8,128)S(1)} %get-tuple-element.23) | copy-start | bytes 1585156
  70.3 26.1 %collective-permute-start.4 = (f32[768,172]{0,1:T(8,128)S(1)}, f32[768,172]{0,1:T(8,128)S(1)}, u32[]{:S(2)}, u32[]{:S(2)}) collective-permute-start(f32[768,172]{0,1:T(8,128)S(1)} %get-tuple-element.23), channel_id=1, source_target_pairs={{0,14},{2,0},{4,2},{6,4},{8,6},{10,8},{12,10},{14,12},{1,15},{3,1}... | collective-permute-start | bytes 1585160 | tf_op jit(solution)/shard_map/ppermute | solution.py:11
  74.8 21.8 %collective-permute-start.5 = (f32[768,172]{0,1:T(8,128)S(1)}, f32[768,172]{0,1:T(8,128)S(1)}, u32[]{:S(2)}, u32[]{:S(2)}) collective-permute-start(f32[768,172]{0,1:T(8,128)S(1)} %get-tuple-element.23), channel_id=1, source_target_pairs={{0,2},{2,4},{4,6},{6,8},{8,10},{10,12},{12,14},{14,0},{1,3},{3,5},... | collective-permute-start | bytes 1585160 | tf_op jit(solution)/shard_map/ppermute | solution.py:11
  74.8 24.2 %collective-permute-start.6 = (f32[768,172]{0,1:T(8,128)S(1)}, f32[768,172]{0,1:T(8,128)S(1)}, u32[]{:S(2)}, u32[]{:S(2)}) collective-permute-start(f32[768,172]{0,1:T(8,128)S(1)} %get-tuple-element.23), channel_id=1, source_target_pairs={{0,12},{2,14},{4,0},{6,2},{8,4},{10,6},{12,8},{14,10},{1,13},{3,15... | collective-permute-start | bytes 1585160 | tf_op jit(solution)/shard_map/ppermute | solution.py:11
  75.9 35.1 %collective-permute-start.7 = (f32[768,172]{0,1:T(8,128)S(1)}, f32[768,172]{0,1:T(8,128)S(1)}, u32[]{:S(2)}, u32[]{:S(2)}) collective-permute-start(f32[768,172]{0,1:T(8,128)S(1)} %get-tuple-element.23), channel_id=1, source_target_pairs={{0,4},{2,6},{4,8},{6,10},{8,12},{10,14},{12,0},{14,2},{1,5},{3,7},... | collective-permute-start | bytes 1585160 | tf_op jit(solution)/shard_map/ppermute | solution.py:11
  77.5 39.2 %copy-start.17 = (s32[1024]{0:T(1024)}, s32[1024]{0:T(1024)S(1)}, u32[]{:S(2)}) copy-start(s32[1024]{0:T(1024)S(1)} %pad_clamp_fusion) | copy-start | bytes 12292
  130.0 11.5 %copy-start.6 = (f32[768,172]{0,1:T(8,128)S(1)}, f32[768,172]{0,1:T(8,128)}, u32[]{:S(2)}) copy-start(f32[768,172]{0,1:T(8,128)} %copy-done.5) | copy-start | bytes 1585156
  130.1 12.5 %copy-start.11 = (s32[768]{0:T(1024)S(1)}, s32[768]{0:T(1024)}, u32[]{:S(2)}) copy-start(s32[768]{0:T(1024)} %param.13) | copy-start | bytes 9220
  131.6 113.7 %reduce-scatter.8.cloned.1.call-start = ((), (), s32[]{:S(2)}) async-start(), calls=%async_computation.5 | async-start | bytes 1622016 | tf_op jit(solution)/shard_map/reduce_scatter | solution.py:103
  142.7 60.7 %copy-start.2 = (f32[768,172]{0,1:T(8,128)}, f32[768,172]{0,1:T(8,128)S(1)}, u32[]{:S(2)}) copy-start(f32[768,172]{0,1:T(8,128)S(1)} %get-tuple-element.26) | copy-start | bytes 1585156
  178.9 34.7 %copy-start.7 = (f32[768,172]{0,1:T(8,128)}, f32[768,172]{0,1:T(8,128)S(1)}, u32[]{:S(2)}) copy-start(f32[768,172]{0,1:T(8,128)S(1)} %get-tuple-element.14) | copy-start | bytes 1585156
  178.9 21.4 %collective-permute-start.8 = (f32[768,172]{0,1:T(8,128)S(1)}, f32[768,172]{0,1:T(8,128)S(1)}, u32[]{:S(2)}, u32[]{:S(2)}) collective-permute-start(f32[768,172]{0,1:T(8,128)S(1)} %get-tuple-element.14), channel_id=1, source_target_pairs={{0,14},{2,0},{4,2},{6,4},{8,6},{10,8},{12,10},{14,12},{1,15},{3,1}... | collective-permute-start | bytes 1585160 | tf_op jit(solution)/shard_map/ppermute | solution.py:11
  179.0 21.4 %collective-permute-start.9 = (f32[768,172]{0,1:T(8,128)S(1)}, f32[768,172]{0,1:T(8,128)S(1)}, u32[]{:S(2)}, u32[]{:S(2)}) collective-permute-start(f32[768,172]{0,1:T(8,128)S(1)} %get-tuple-element.14), channel_id=1, source_target_pairs={{0,2},{2,4},{4,6},{6,8},{8,10},{10,12},{12,14},{14,0},{1,3},{3,5},... | collective-permute-start | bytes 1585160 | tf_op jit(solution)/shard_map/ppermute | solution.py:11
  181.0 22.3 %collective-permute-start.10 = (f32[768,172]{0,1:T(8,128)S(1)}, f32[768,172]{0,1:T(8,128)S(1)}, u32[]{:S(2)}, u32[]{:S(2)}) collective-permute-start(f32[768,172]{0,1:T(8,128)S(1)} %get-tuple-element.14), channel_id=1, source_target_pairs={{0,12},{2,14},{4,0},{6,2},{8,4},{10,6},{12,8},{14,10},{1,13},{3,15... | collective-permute-start | bytes 1585160 | tf_op jit(solution)/shard_map/ppermute | solution.py:11
  181.0 32.6 %collective-permute-start.11 = (f32[768,172]{0,1:T(8,128)S(1)}, f32[768,172]{0,1:T(8,128)S(1)}, u32[]{:S(2)}, u32[]{:S(2)}) collective-permute-start(f32[768,172]{0,1:T(8,128)S(1)} %get-tuple-element.14), channel_id=1, source_target_pairs={{0,4},{2,6},{4,8},{6,10},{8,12},{10,14},{12,0},{14,2},{1,5},{3,7},... | collective-permute-start | bytes 1585160 | tf_op jit(solution)/shard_map/ppermute | solution.py:11
  223.0 6.0 %copy-start.14 = (s32[1,1,70]{2,1,0:T(1,128)S(1)}, s32[1,1,70]{2,1,0:T(1,128)}, u32[]{:S(2)}) copy-start(s32[1,1,70]{2,1,0:T(1,128)} %param.17) | copy-start | bytes 844
  232.8 12.5 %copy-start.8 = (f32[768,172]{0,1:T(8,128)S(1)}, f32[768,172]{0,1:T(8,128)}, u32[]{:S(2)}) copy-start(f32[768,172]{0,1:T(8,128)} %copy-done.7) | copy-start | bytes 1585156
  232.9 13.5 %copy-start.4 = (bf16[768,256]{1,0:T(8,128)(2,1)S(1)}, bf16[768,256]{1,0:T(8,128)(2,1)}, u32[]{:S(2)}) copy-start(bf16[768,256]{1,0:T(8,128)(2,1)} %copy-done.3) | copy-start | bytes 1179652
  234.4 105.1 %all-reduce.5.cloned.1.call-start = ((), (), s32[]{:S(2)}) async-start(), calls=%async_computation.6 | async-start | bytes 622592 | tf_op jit(solution)/shard_map/psum | solution.py:116
  (4 other events, 13.6 us)
Sparse Core Ops, SparseCore 0:
  60.1 8.3 reduce-scatter.3
  131.7 9.7 reduce-scatter.5
  234.5 10.7 reduce-scatter.7
  249.5 89.8 all-reduce.4
where the time goes:
time: 351 us; the launch traced here: 350 us
  waiting for transfers between devices  193 us (55%)
  local copies, waits for them, and re-layouts  38.3 us (11%)
  blocking collectives  37 us (11%)
  matrix products  34.7 us (10%)
  starting transfers between devices  20.7 us (6%)
  between operations  17.9 us (5%)
  other arithmetic  9.16 us (3%)
    psum x1, waiting for transfers between devices, shards(): grad_one = lax.psum(grad_one, ('row', 'col'))  89.6 us
    ppermute x12, waiting for transfers between devices, from_behind(): lax.ppermute(value, axis, [(i, (i + by) % peers) for i in range(peers)])  77.6 us
    psum x1, blocking collectives, shards(): lax.psum((loss_local, jnp.sum(train_f)), ('row', 'col'))  34.6 us
    ppermute x12, starting transfers between devices, from_behind(): lax.ppermute(value, axis, [(i, (i + by) % peers) for i in range(peers)])  20.5 us
    dot_general x3, matrix products, spread(): jnp.einsum('tuv,tvw->tuw', tiles_wide, picked, preferred_element_type=jnp...  17.2 us
    unnamed x57, local copies, waits for them, and re-layouts  13.2 us
    gather x3, local copies, waits for them, and re-layouts, spread(): picked = jnp.take(buffer_rows, slot_index, axis=0)  11.9 us
    dot_general x3, matrix products, spread(): jnp.einsum('ta,tuw->auw', row_weights, product, precision=lax.Precision.H...  11.8 us
  transfers between devices with their start and end apart: 16, of which 13 were waited for; matrix products, arithmetic and copies ran while one was open for 4% of the time, Pallas kernels for 0%

commit v1 on v0

v1 whole, which is shorter than its diff:
```python
import functools

import jax
import jax.numpy as jnp
from jax import lax
from jax.experimental import pallas as pl
from jax.experimental.pallas import tpu as pltpu
from jax.sharding import PartitionSpec as P

TILE = 128
MESH = pl.DeviceIdType.MESH
F32 = jnp.float32
BF16 = jnp.bfloat16


def ceil_to(value, unit):
    return -(-value // unit) * unit


def reduce_plan(rows, row_total):
    levels = [("col", 1)]
    bit = 1
    while bit < row_total:
        levels.append(("row", bit))
        bit *= 2
    plan = []
    for axis, bit in levels:
        halved = rows % 16 == 0
        rows = rows // 2 if halved else rows
        plan.append((axis, bit, rows, halved))
    return plan


def kernel(
    row_total, classes, plan,
    map_ref, feat_ref, w1t_ref, w2t_ref, w2_ref, lab_ref, mask_ref, esrc_ref, edst_ref,
    logits_out, g1_out, g2_out, loss_out,
    tiles, adj, x1, x2, x3, acc, rx1, rx2, rx3, hid, cnt, cnt_rx, grads, gathered, *rest,
):
    grad_rx = rest[: len(plan)]
    halo_send, halo_recv, col_send, col_recv, cnt_send, cnt_recv, sum_send, sum_recv, all_send, all_recv = rest[len(plan):]
    quarter = row_total // 4
    offsets = [0, 1, -1, quarter, -quarter]
    sources = len(offsets)
    here = lax.axis_index("row")
    col = lax.axis_index("col")
    other = 1 - col
    f_in, nodes = feat_ref.shape
    width = w2t_ref.shape[0]
    hidden_total = w1t_ref.shape[0]
    owned = nodes // TILE
    slots = esrc_ref.shape[0]

    def level_peer(axis, bit):
        if axis == "col":
            return {"col": other}
        is_set = (here // bit) % 2
        return {"row": here + bit - 2 * bit * is_set}

    def level_bit(axis, bit):
        return col if axis == "col" else (here // bit) % 2

    halo_peers = [None] + [
        {"row": lax.rem(here - off + row_total, row_total)} for off in offsets[1:]
    ]
    greet = halo_peers[1:] + [level_peer(axis, bit) for axis, bit, _, _ in plan]
    barrier = pltpu.get_barrier_semaphore()
    for peer in greet:
        pl.semaphore_signal(barrier, inc=1, device_id=peer, device_id_type=MESH)
    x1[0] = feat_ref[...]
    cnt[...] = jnp.zeros(cnt.shape, F32) + jnp.sum(mask_ref[...].astype(F32))
    pl.semaphore_wait(barrier, len(greet))

    pending = []

    def remote(src, dst, send, recv, peer):
        return pltpu.make_async_remote_copy(
            src_ref=src, dst_ref=dst, send_sem=send, recv_sem=recv,
            device_id=peer, device_id_type=MESH,
        )

    def start_halo(phase, buf):
        for p in range(sources - 1, 0, -1):
            copy = remote(
                buf.at[0], buf.at[p], halo_send.at[phase, p], halo_recv.at[phase, p], halo_peers[p]
            )
            copy.start()
            pending.append(copy)

    def wait_halo(phase, buf, p):
        remote(
            buf.at[0], buf.at[p], halo_send.at[phase, p], halo_recv.at[phase, p], {"col": other}
        ).wait_recv()

    def count_levels():
        for k, (axis, bit, _, _) in enumerate(plan):
            copy = remote(
                cnt, cnt_rx.at[k], cnt_send.at[k], cnt_recv.at[k], level_peer(axis, bit)
            )
            copy.start()
            yield
            copy.wait()
            cnt[...] += cnt_rx[k]

    counter = count_levels()
    next(counter, None)
    start_halo(0, x1)

    sub_ids = lax.broadcasted_iota(jnp.int32, (TILE, TILE), 0)
    one, zero = jnp.ones((TILE, TILE), F32), jnp.zeros((TILE, TILE), F32)

    def build(t, carry):
        src = jnp.where(sub_ids == esrc_ref[pl.ds(t, 1), :], one, zero).astype(BF16)
        dst = jnp.where(sub_ids == edst_ref[pl.ds(t, 1), :], one, zero).astype(BF16)
        tiles[t] = lax.dot_general(
            src, dst, (((1,), (1,)), ((), ())), preferred_element_type=F32
        ).astype(BF16)
        return carry

    lax.fori_loop(0, slots, build, 0, unroll=2)
    tiles[slots] = jnp.zeros((TILE, TILE), BF16)
    next(counter, None)

    def place(p, carry):
        for k in range(owned):
            for a in range(2 * owned):
                index = map_ref[(p * owned + k) * 2 * owned + a]
                adj[a // owned, p, k * TILE:(k + 1) * TILE,
                    (a % owned) * TILE:(a % owned + 1) * TILE] = tiles[index]
        return carry

    lax.fori_loop(0, sources, place, 0)
    next(counter, None)

    def aggregate(phase, buf, lhs, rows, rx):
        part = acc.at[:, 0:rows, :]
        part[...] = jnp.zeros(part.shape, F32)

        def step(p, carry):
            @pl.when(p > 0)
            def _():
                wait_halo(phase, buf, p)

            x = lhs(p)
            for d in range(2):
                part[d] += jnp.dot(x, adj[d, p], preferred_element_type=F32)
            return carry

        lax.fori_loop(0, sources - 1, step, 0)
        last = sources - 1
        wait_halo(phase, buf, last)
        x = lhs(last)
        part[other] += jnp.dot(x, adj[other, last], preferred_element_type=F32)
        copy = remote(
            part.at[other], rx, col_send.at[phase], col_recv.at[phase], {"col": other}
        )
        copy.start()
        part[col] += jnp.dot(x, adj[col, last], preferred_element_type=F32)
        copy.wait()
        return part[col] + rx[...]

    ones = jnp.ones((16, nodes), BF16)
    total = aggregate(
        0, x1, lambda p: jnp.concatenate([x1[p].astype(BF16), ones], axis=0), f_in + 16, rx1
    )
    degree = 1.0 + total[f_in:f_in + 1]
    agg = ((total[:f_in] + x1[0]) / degree).astype(BF16)
    x2[0] = agg.astype(F32)
    start_halo(1, x2)
    next(counter, None)

    def hidden_of(p):
        return jnp.maximum(
            jnp.dot(w1t_ref[...], x2[p].astype(BF16), preferred_element_type=F32), 0.0
        ).astype(BF16)

    def projected_of(p):
        return jnp.dot(w2t_ref[...], hidden_of(p), preferred_element_type=F32)

    hid[...] = hidden_of(0)
    logit_sum = aggregate(1, x2, lambda p: projected_of(p).astype(BF16), width, rx2)
    for _ in counter:
        pass
    train_count = cnt[0:1, 0:1]
    projected = jnp.dot(w2t_ref[...], hid[...], preferred_element_type=F32)
    logits = (logit_sum + projected) / degree
    logits_out[...] = logits
    class_ids = lax.broadcasted_iota(jnp.int32, (width, nodes), 0)
    masked = jnp.where(class_ids < classes, logits, -jnp.inf)
    row_max = jnp.max(masked, axis=0, keepdims=True)
    log_total = row_max + jnp.log(jnp.sum(jnp.exp(masked - row_max), axis=0, keepdims=True))
    hit = class_ids == lab_ref[...]
    train_f = mask_ref[...].astype(F32)
    probabilities = jnp.exp(masked - log_total)
    logit_grad = train_f * (probabilities - jnp.where(hit, 1.0, 0.0)) / train_count
    error = (logit_grad / degree).astype(BF16)
    x3[0] = error.astype(F32)
    start_halo(2, x3)
    picked = jnp.sum(jnp.where(hit, logits, 0.0), axis=0, keepdims=True)
    loss_local = jnp.sum(train_f * (log_total - picked))

    back_sum = aggregate(2, x3, lambda p: x3[p].astype(BF16), width, rx3)
    proj_grad = (back_sum + x3[0]).astype(BF16)
    contract_nodes = (((1,), (1,)), ((), ()))
    grad_two = lax.dot_general(proj_grad, hid[...], contract_nodes, preferred_element_type=F32)
    hidden_grad = jnp.dot(w2_ref[...], proj_grad, preferred_element_type=F32)
    active = jnp.where(hid[...].astype(F32) > 0, hidden_grad, 0.0).astype(BF16)
    grad_one = lax.dot_general(
        x2[0].astype(BF16), active, contract_nodes, preferred_element_type=F32
    )
    spots = []
    at = 0
    for grad, out in ((grad_one, g1_out), (grad_two, g2_out)):
        for lane in range(0, hidden_total, TILE):
            grads[at:at + grad.shape[0], :] = grad[:, lane:lane + TILE]
            spots.append((at, grad.shape[0], out, lane))
            at += grad.shape[0]
    grads[at:, :] = jnp.zeros((grads.shape[0] - at, TILE), F32) + loss_local

    base = 0
    bases = []
    for k, (axis, bit, rows, halved) in enumerate(plan):
        peer = level_peer(axis, bit)
        mine = level_bit(axis, bit)
        bases.append(base)
        if halved:
            keep = pl.multiple_of(base + mine * rows, 8)
            away = pl.multiple_of(base + (1 - mine) * rows, 8)
        else:
            keep = away = base
        copy = remote(
            grads.at[pl.ds(away, rows), :], grad_rx[k], sum_send.at[k], sum_recv.at[k], peer
        )
        copy.start()
        copy.wait()
        grads[pl.ds(keep, rows), :] += grad_rx[k][...]
        base = keep
    rows = plan[-1][2]
    gathered[pl.ds(base, rows), :] = grads[pl.ds(base, rows), :]
    for k in range(len(plan) - 1, -1, -1):
        axis, bit, rows, halved = plan[k]
        if not halved:
            continue
        mine = level_bit(axis, bit)
        piece = gathered.at[pl.ds(pl.multiple_of(bases[k] + mine * rows, 8), rows), :]
        copy = remote(piece, piece, all_send.at[k], all_recv.at[k], level_peer(axis, bit))
        copy.start()
        copy.wait()
    for start, count, out, lane in spots:
        out[:, lane:lane + TILE] = gathered[start:start + count, :]
    loss_out[...] = gathered[at:at + 8, :] / cnt[...]
    for copy in pending:
        copy.wait_send()


def shards(
    row_total, features, labels, train_mask, w_one, w_two, tile_rows, tile_cols, tile_count,
    edge_dst, edge_src,
):
    nodes, f_in = features.shape
    owned = nodes // TILE
    hidden_total, classes = w_two.shape
    width = ceil_to(classes, 16)
    quarter = row_total // 4
    here = lax.axis_index("row")
    offsets = [0, 1, -1, quarter, -quarter]
    sources = len(offsets)
    slot_rows, slot_cols = tile_rows[0, 0], tile_cols[0, 0]
    slots = slot_rows.shape[0]
    slot_ids = lax.iota(jnp.int32, slots)
    distance = (slot_cols // owned - here) % row_total
    position = sum(
        p * (distance == off % row_total).astype(jnp.int32) for p, off in enumerate(offsets)
    )
    spot = (position * owned + slot_cols % owned) * 2 * owned + slot_rows
    spot = jnp.where(slot_ids < tile_count[0, 0], spot, -1)
    spots_total = sources * owned * 2 * owned
    slot_map = slots + jnp.sum(
        jnp.where(lax.iota(jnp.int32, spots_total)[:, None] == spot[None, :], slot_ids - slots, 0),
        axis=1,
    )
    feat_t = features.T.astype(F32)
    w2 = jnp.pad(w_two, ((0, 0), (0, width - classes)))
    grad_rows = (f_in + width) * (hidden_total // TILE)
    grad_rows = ceil_to(grad_rows + 8, 128)
    plan = reduce_plan(grad_rows, row_total)
    levels = len(plan)
    vmem = pl.BlockSpec(memory_space=pltpu.VMEM)
    dma = pltpu.SemaphoreType.DMA
    logits_t, grad_one, grad_two_t, loss = pl.pallas_call(
        functools.partial(kernel, row_total, classes, plan),
        out_shape=(
            jax.ShapeDtypeStruct((width, nodes), F32),
            jax.ShapeDtypeStruct((f_in, hidden_total), F32),
            jax.ShapeDtypeStruct((width, hidden_total), F32),
            jax.ShapeDtypeStruct((8, TILE), F32),
        ),
        in_specs=[pl.BlockSpec(memory_space=pltpu.SMEM)] + [vmem] * 8,
        out_specs=[vmem] * 4,
        scratch_shapes=[
            pltpu.VMEM((slots + 1, TILE, TILE), BF16),
            pltpu.VMEM((2, sources, nodes, nodes), BF16),
            pltpu.VMEM((sources, f_in, nodes), F32),
            pltpu.VMEM((sources, f_in, nodes), F32),
            pltpu.VMEM((sources, width, nodes), F32),
            pltpu.VMEM((2, max(width, f_in + 16), nodes), F32),
            pltpu.VMEM((f_in + 16, nodes), F32),
            pltpu.VMEM((width, nodes), F32),
            pltpu.VMEM((width, nodes), F32),
            pltpu.VMEM((hidden_total, nodes), BF16),
            pltpu.VMEM((8, TILE), F32),
            pltpu.VMEM((levels, 8, TILE), F32),
            pltpu.VMEM((grad_rows, TILE), F32),
            pltpu.VMEM((grad_rows, TILE), F32),
        ]
        + [pltpu.VMEM((rows, TILE), F32) for _, _, rows, _ in plan]
        + [dma((3, sources)), dma((3, sources)), dma((3,)), dma((3,))]
        + [dma((levels,)) for _ in range(6)],
        compiler_params=pltpu.CompilerParams(
            collective_id=0, has_side_effects=True, vmem_limit_bytes=48 * 1024 * 1024
        ),
    )(
        slot_map, feat_t, w_one.T, w2.T, w2, labels.reshape(1, -1), train_mask.reshape(1, -1),
        edge_src[0, 0], edge_dst[0, 0],
    )
    return (
        logits_t[:classes].T,
        loss[0, :1],
        grad_one,
        grad_two_t[:classes].T,
    )


def solution(mesh):
    nodes = P(("parts", "row", "col"))
    return jax.shard_map(
        functools.partial(shards, mesh.shape["row"]),
        mesh=mesh,
        in_specs=(
            P(("parts", "row", "col"), None),
            nodes,
            nodes,
            P(),
            P(),
            P(("parts", "row"), "col", None),
            P(("parts", "row"), "col", None),
            P(("parts", "row"), "col"),
            P(("parts", "row"), "col", None, None),
            P(("parts", "row"), "col", None, None),
        ),
        out_specs=(
            P(("parts", "row", "col"), None),
            P("parts"),
            P("parts", None),
            P("parts", None),
        ),
        check_vma=False,
    )
```

time: 351 us -> 145 us (0.41)
  waiting for transfers between devices: 193 us -> 0 us
  Pallas kernels: 0 us -> 136 us
  blocking collectives: 37 us -> 0 us
  matrix products: 34.7 us -> 0 us
  local copies, waits for them, and re-layouts: 38.3 us -> 7.61 us
  starting transfers between devices: 20.7 us -> 0 us
  between operations: 17.9 us -> 1.41 us
  other arithmetic: 9.16 us -> 0.16 us
    pallas_call x0 -> x1, Pallas kernels: none -> 136 us  [shards(): pl.pallas_call(functools.partial(kernel, row_total, classes, plan), out_s...]
    psum x1 -> x0, waiting for transfers between devices: 89.6 us -> none  [shards(): grad_one = lax.psum(grad_one, ('row', 'col'))]
    ppermute x12 -> x0, waiting for transfers between devices: 77.6 us -> none  [from_behind(): lax.ppermute(value, axis, [(i, (i + by) % peers) for i in range(peers)])]
    dot_general x12 -> x0, matrix products: 34.7 us -> none  [the longest x3 17.2 us: spread(): jnp.einsum('tuv,tvw->tuw', tiles_wide, picked, preferred_element_type=jnp...]
    psum x1 -> x0, blocking collectives: 34.6 us -> none  [shards(): lax.psum((loss_local, jnp.sum(train_f)), ('row', 'col'))]
    reduce_scatter x3 -> x0, waiting for transfers between devices: 25.3 us -> none  [the longest x1 10.9 us: shards(): lax.psum_scatter(error_terms, 'col', scatter_dimension=0, tiled=True)]
    ppermute x12 -> x0, starting transfers between devices: 20.5 us -> none  [from_behind(): lax.ppermute(value, axis, [(i, (i + by) % peers) for i in range(peers)])]
    gather x3 -> x0, local copies, waits for them, and re-layouts: 11.9 us -> none  [spread(): picked = jnp.take(buffer_rows, slot_index, axis=0)]
  transfers between devices with their start and end apart: 16 -> 0, of which waited for: 13 -> 0; matrix products, arithmetic and copies ran while one was open for 4% -> 0% of each run, Pallas kernels for 0% -> 0%
where the time goes in v1:
time: 145 us
  Pallas kernels  136 us (94%)
  local copies, waits for them, and re-layouts  7.61 us (5%)
    pallas_call x1, Pallas kernels, shards(): pl.pallas_call(functools.partial(kernel, row_total, classes, plan), out_s...  136 us
    unnamed x21, local copies, waits for them, and re-layouts  5.45 us

profile of v1, /device:TPU:0, one launch (start us, length us, event | category | flops | bytes accessed | tf_op | source)
XLA Modules:
  0.0 145.1 jit_solution(13937493165352942771)
XLA Ops:
  1.3 0.0 copy-start.6
  1.3 0.0 copy-start.7
  1.3 0.6 copy-done.6
  1.9 0.0 copy-done.7
  2.0 0.0 copy-start.4
  2.0 0.1 select_reduce_fusion
  2.1 0.6 copy-done.4
  2.7 0.0 copy-start.5
  2.7 0.7 copy-done.5
  3.4 0.0 copy-start.2
  3.4 0.0 copy-start.3
  3.4 1.0 copy.19
  4.3 0.0 copy-start.1
  4.3 0.0 copy-done.2
  4.3 0.0 copy-done.3
  4.4 0.8 copy-done.1
  5.2 0.1 copy.20
  5.4 0.0 copy-start
  5.4 0.1 copy.21.w2t_ref
  5.5 0.8 copy-done
  6.3 0.1 copy.18
  6.5 135.9 %shard_map.129 = (f32[176,768]{1,0:T(8,128)S(1)}, f32[128,256]{1,0:T(8,128)S(1)}, f32[176,256]{1,0:T(8,128)S(1)}, f32[8,128]{1,0:T(8,128)S(1)}) custom-call(s32[360]{0:T(512)S(1)} %broadcast_add_fusion.map_ref, f32[128,768]{1,0:T(8,128)S(1)} %convert_bitcast_fusion.feat_ref, bf16[256,128]{1,0:T(8,128)(2,1)S(1)} %bitcast.37, ...), custom_call_target="tpu_custom_call" | custom-call | tf_op jit(solution)/shard_map/pallas_call | solution.py:290
  142.4 0.5 slice.10
  142.9 0.8 slice_bitcast_fusion
  143.7 0.7 slice_bitcast_fusion.1
  144.4 0.7 copy.28
  (7 shorter events, 0.1 us)
Async XLA Ops:
  1.3 0.7 copy-start.6
  1.3 0.7 copy-start.7
  2.0 0.7 copy-start.4
  2.7 0.7 copy-start.5
  3.4 1.0 copy-start.2
  3.4 1.0 copy-start.3
  4.3 0.9 copy-start.1
  5.4 0.9 copy-start

commit v2 on v1

--- a/solution.py
+++ b/solution.py
@@ -15,6 +15,20 @@
 
 def ceil_to(value, unit):
     return -(-value // unit) * unit
+
+
+def pieces(rows, count):
+    units = rows // 8
+    cuts = [8 * (units * k // count) for k in range(count + 1)]
+    return [(lo, hi - lo) for lo, hi in zip(cuts, cuts[1:])]
+
+
+CHUNKS = 4
+
+
+def source_offsets(row_total):
+    quarter = row_total // 4
+    return [0, 1, quarter, -quarter, -1]
 
 
 def reduce_plan(rows, row_total):
@@ -39,10 +53,18 @@
 ):
     grad_rx = rest[: len(plan)]
     halo_send, halo_recv, col_send, col_recv, cnt_send, cnt_recv, sum_send, sum_recv, all_send, all_recv = rest[len(plan):]
-    quarter = row_total // 4
-    offsets = [0, 1, -1, quarter, -quarter]
+    offsets = source_offsets(row_total)
     sources = len(offsets)
     here = lax.axis_index("row")
+    sign = 1 - 2 * (here % 2)
+    forwards = row_total // 4 == 2
+    wraps = []
+    for off in offsets[2:4]:
+        lap = (here + sign * off + row_total) // row_total - 1
+        wraps.append(lap * lap)
+    third = 2 + wraps[0]
+    fourth = 3 - wraps[0] + wraps[1]
+    fifth = 4 - wraps[1]
     col = lax.axis_index("col")
     other = 1 - col
     f_in, nodes = feat_ref.shape
@@ -60,9 +82,12 @@
     def level_bit(axis, bit):
         return col if axis == "col" else (here // bit) % 2
 
-    halo_peers = [None] + [
-        {"row": lax.rem(here - off + row_total, row_total)} for off in offsets[1:]
-    ]
+    def row_at(off):
+        return {"row": lax.rem(here + sign * off + row_total, row_total)}
+
+    quarter_flip = (row_total // 4) % 2
+    near, far = (offsets[2], offsets[3]) if quarter_flip else (offsets[3], offsets[2])
+    halo_peers = [None, row_at(1), row_at(near), row_at(far), row_at(-1)]
     greet = halo_peers[1:] + [level_peer(axis, bit) for axis, bit, _, _ in plan]
     barrier = pltpu.get_barrier_semaphore()
     for peer in greet:
@@ -79,18 +104,31 @@
             device_id=peer, device_id_type=MESH,
         )
 
+    def halo_copy(phase, buf, source, p, k, peer):
+        lo, rows = pieces(buf.shape[1], CHUNKS)[k]
+        return remote(
+            buf.at[source, pl.ds(lo, rows), :], buf.at[p, pl.ds(lo, rows), :],
+            halo_send.at[phase, p, k], halo_recv.at[phase, p, k], peer,
+        )
+
     def start_halo(phase, buf):
-        for p in range(sources - 1, 0, -1):
-            copy = remote(
-                buf.at[0], buf.at[p], halo_send.at[phase, p], halo_recv.at[phase, p], halo_peers[p]
+        for p in (2, 1, 3) if forwards else (2, 1, 3, 4):
+            for k in range(CHUNKS):
+                copy = halo_copy(phase, buf, 0, p, k, halo_peers[p])
+                copy.start()
+                pending.append(copy)
+        if forwards:
+            pending.extend(
+                halo_copy(phase, buf, 2, 4, k, halo_peers[1]) for k in range(CHUNKS)
             )
-            copy.start()
-            pending.append(copy)
 
     def wait_halo(phase, buf, p):
-        remote(
-            buf.at[0], buf.at[p], halo_send.at[phase, p], halo_recv.at[phase, p], {"col": other}
-        ).wait_recv()
+        for k in range(CHUNKS):
+            halo_copy(phase, buf, 0, p, k, {"col": other}).wait_recv()
+            if forwards:
+                @pl.when(p == 2)
+                def _():
+                    halo_copy(phase, buf, 2, 4, k, halo_peers[1]).start()
 
     def count_levels():
         for k, (axis, bit, _, _) in enumerate(plan):
@@ -136,8 +174,10 @@
         part = acc.at[:, 0:rows, :]
         part[...] = jnp.zeros(part.shape, F32)
 
-        def step(p, carry):
-            @pl.when(p > 0)
+        def step(i, carry):
+            p = jnp.where(i == 2, third, jnp.where(i == 3, fourth, i))
+
+            @pl.when(i > 0)
             def _():
                 wait_halo(phase, buf, p)
 
@@ -147,7 +187,7 @@
             return carry
 
         lax.fori_loop(0, sources - 1, step, 0)
-        last = sources - 1
+        last = fifth
         wait_halo(phase, buf, last)
         x = lhs(last)
         part[other] += jnp.dot(x, adj[other, last], preferred_element_type=F32)
@@ -261,16 +301,16 @@
     owned = nodes // TILE
     hidden_total, classes = w_two.shape
     width = ceil_to(classes, 16)
-    quarter = row_total // 4
     here = lax.axis_index("row")
-    offsets = [0, 1, -1, quarter, -quarter]
+    sign = 1 - 2 * (here % 2)
+    offsets = source_offsets(row_total)
     sources = len(offsets)
     slot_rows, slot_cols = tile_rows[0, 0], tile_cols[0, 0]
     slots = slot_rows.shape[0]
     slot_ids = lax.iota(jnp.int32, slots)
     distance = (slot_cols // owned - here) % row_total
     position = sum(
-        p * (distance == off % row_total).astype(jnp.int32) for p, off in enumerate(offsets)
+        p * (distance == (sign * off) % row_total).astype(jnp.int32) for p, off in enumerate(offsets)
     )
     spot = (position * owned + slot_cols % owned) * 2 * owned + slot_rows
     spot = jnp.where(slot_ids < tile_count[0, 0], spot, -1)
@@ -314,7 +354,7 @@
             pltpu.VMEM((grad_rows, TILE), F32),
         ]
         + [pltpu.VMEM((rows, TILE), F32) for _, _, rows, _ in plan]
-        + [dma((3, sources)), dma((3, sources)), dma((3,)), dma((3,))]
+        + [dma((3, sources, CHUNKS)), dma((3, sources, CHUNKS)), dma((3,)), dma((3,))]
         + [dma((levels,)) for _ in range(6)],
         compiler_params=pltpu.CompilerParams(
             collective_id=0, has_side_effects=True, vmem_limit_bytes=48 * 1024 * 1024

time: 145 us -> 131 us (0.903)
  Pallas kernels: 136 us -> 122 us
    pallas_call x1, Pallas kernels: 136 us -> 122 us  [shards(): pl.pallas_call(functools.partial(kernel, row_total, classes, plan), out_s...]
    unnamed x21 -> x23, local copies, waits for them, and re-layouts: 5.45 us -> 4.64 us
where the time goes in v2:
time: 131 us; the launch traced here: 130 us
  Pallas kernels  122 us (93%)
  local copies, waits for them, and re-layouts  6.8 us (5%)
  between operations  1.48 us (1%)
    pallas_call x1, Pallas kernels, shards(): pl.pallas_call(functools.partial(kernel, row_total, classes, plan), out_s...  122 us
    unnamed x23, local copies, waits for them, and re-layouts  4.64 us

profile of v2, /device:TPU:0, one launch (start us, length us, event | category | flops | bytes accessed | tf_op | source)
XLA Modules:
  0.0 130.3 jit_solution(7158019374788239777)
XLA Ops:
  0.6 0.0 copy-start.2
  1.4 0.0 copy-start.7
  1.4 0.0 copy-start.8
  1.4 0.6 copy-done.7
  2.0 0.0 copy-done.8
  2.1 0.0 copy-start.5
  2.1 0.1 select_reduce_fusion
  2.2 0.6 copy-done.5
  2.8 0.0 copy-start.6
  2.8 0.7 copy-done.6
  3.4 0.0 copy-done.2
  3.4 0.0 copy-start.3
  3.5 0.0 copy-start.4
  3.5 0.1 copy.19
  3.6 0.0 copy-start.1
  3.6 0.6 copy-done.3
  4.2 0.0 copy-done.4
  4.2 0.2 copy-done.1
  4.5 0.1 copy.20
  4.6 0.0 copy-start
  4.6 0.1 copy.21.w2t_ref
  4.7 0.8 copy-done
  5.6 0.1 copy.18
  5.7 121.9 %shard_map.129 = (f32[176,768]{1,0:T(8,128)S(1)}, f32[128,256]{1,0:T(8,128)S(1)}, f32[176,256]{1,0:T(8,128)S(1)}, f32[8,128]{1,0:T(8,128)S(1)}) custom-call(s32[360]{0:T(512)S(1)} %broadcast_add_fusion.map_ref, f32[128,768]{1,0:T(8,128)S(1)} %convert_bitcast_fusion.feat_ref, bf16[256,128]{1,0:T(8,128)(2,1)S(1)} %bitcast.37, ...), custom_call_target="tpu_custom_call" | custom-call | tf_op jit(solution)/shard_map/pallas_call | solution.py:330
  127.6 0.5 slice.10
  128.2 0.8 slice_bitcast_fusion
  129.0 0.7 slice_bitcast_fusion.1
  129.7 0.7 copy.28
  (7 shorter events, 0.1 us)
Async XLA Ops:
  0.6 2.8 %copy-start.2 = (bf16[128,256]{1,0:T(8,128)(2,1)S(1)}, bf16[128,256]{1,0:T(8,128)(2,1)}, u32[]{:S(2)}) copy-start(bf16[128,256]{1,0:T(8,128)(2,1)} %param.13) | copy-start | bytes 196612
  1.4 0.7 copy-start.7
  1.4 0.7 copy-start.8
  2.1 0.7 copy-start.5
  2.8 0.7 copy-start.6
  3.4 0.8 copy-start.3
  3.5 0.8 copy-start.4
  3.6 0.9 copy-start.1
  4.6 0.9 copy-start

commit v3 on v2

--- a/solution.py
+++ b/solution.py
@@ -51,20 +51,14 @@
     logits_out, g1_out, g2_out, loss_out,
     tiles, adj, x1, x2, x3, acc, rx1, rx2, rx3, hid, cnt, cnt_rx, grads, gathered, *rest,
 ):
-    grad_rx = rest[: len(plan)]
-    halo_send, halo_recv, col_send, col_recv, cnt_send, cnt_recv, sum_send, sum_recv, all_send, all_recv = rest[len(plan):]
+    buffers = 2 if row_total <= 8 else len(plan)
+    grad_rx = rest[:buffers]
+    halo_send, halo_recv, col_send, col_recv, cnt_send, cnt_recv, sum_send, sum_recv, all_send, all_recv = rest[buffers:]
     offsets = source_offsets(row_total)
     sources = len(offsets)
     here = lax.axis_index("row")
     sign = 1 - 2 * (here % 2)
     forwards = row_total // 4 == 2
-    wraps = []
-    for off in offsets[2:4]:
-        lap = (here + sign * off + row_total) // row_total - 1
-        wraps.append(lap * lap)
-    third = 2 + wraps[0]
-    fourth = 3 - wraps[0] + wraps[1]
-    fifth = 4 - wraps[1]
     col = lax.axis_index("col")
     other = 1 - col
     f_in, nodes = feat_ref.shape
@@ -88,7 +82,15 @@
     quarter_flip = (row_total // 4) % 2
     near, far = (offsets[2], offsets[3]) if quarter_flip else (offsets[3], offsets[2])
     halo_peers = [None, row_at(1), row_at(near), row_at(far), row_at(-1)]
-    greet = halo_peers[1:] + [level_peer(axis, bit) for axis, bit, _, _ in plan]
+    direct = row_total <= 8
+    everyone = [
+        {"row": lax.rem(here + by, row_total), "col": col if side == 0 else other}
+        for by in range(row_total) for side in range(2)
+    ][1:] if direct else []
+    if direct:
+        greet = everyone
+    else:
+        greet = halo_peers[1:] + [level_peer(axis, bit) for axis, bit, _, _ in plan]
     barrier = pltpu.get_barrier_semaphore()
     for peer in greet:
         pl.semaphore_signal(barrier, inc=1, device_id=peer, device_id_type=MESH)
@@ -111,24 +113,27 @@
             halo_send.at[phase, p, k], halo_recv.at[phase, p, k], peer,
         )
 
-    def start_halo(phase, buf):
-        for p in (2, 1, 3) if forwards else (2, 1, 3, 4):
+    def start_halo(phase, buf, sources=(2, 1) if forwards else (2, 1, 3, 4)):
+        for p in sources:
             for k in range(CHUNKS):
                 copy = halo_copy(phase, buf, 0, p, k, halo_peers[p])
                 copy.start()
                 pending.append(copy)
-        if forwards:
-            pending.extend(
-                halo_copy(phase, buf, 2, 4, k, halo_peers[1]) for k in range(CHUNKS)
-            )
+
+    def forward_halo(phase, buf):
+        for k in range(CHUNKS):
+            halo_copy(phase, buf, 0, 2, k, halo_peers[2]).wait_recv()
+            copy = halo_copy(phase, buf, 2, 4, k, halo_peers[1])
+            copy.start()
+            pending.append(copy)
+        for copy in pending[-3 * CHUNKS:-2 * CHUNKS]:
+            copy.wait_send()
+        del pending[-3 * CHUNKS:-2 * CHUNKS]
+        start_halo(phase, buf, (3,))
 
     def wait_halo(phase, buf, p):
         for k in range(CHUNKS):
             halo_copy(phase, buf, 0, p, k, {"col": other}).wait_recv()
-            if forwards:
-                @pl.when(p == 2)
-                def _():
-                    halo_copy(phase, buf, 2, 4, k, halo_peers[1]).start()
 
     def count_levels():
         for k, (axis, bit, _, _) in enumerate(plan):
@@ -140,9 +145,16 @@
             copy.wait()
             cnt[...] += cnt_rx[k]
 
-    counter = count_levels()
+    counter = iter(()) if direct else count_levels()
+    start_halo(0, x1)
+    if direct:
+        counts = [
+            remote(cnt, cnt_rx.at[k], cnt_send.at[k], cnt_recv.at[k], peer)
+            for k, peer in enumerate(everyone)
+        ]
+        for copy in counts:
+            copy.start()
     next(counter, None)
-    start_halo(0, x1)
 
     sub_ids = lax.broadcasted_iota(jnp.int32, (TILE, TILE), 0)
     one, zero = jnp.ones((TILE, TILE), F32), jnp.zeros((TILE, TILE), F32)
@@ -174,20 +186,28 @@
         part = acc.at[:, 0:rows, :]
         part[...] = jnp.zeros(part.shape, F32)
 
-        def step(i, carry):
-            p = jnp.where(i == 2, third, jnp.where(i == 3, fourth, i))
-
-            @pl.when(i > 0)
-            def _():
+        def step(p, carry):
+            if forwards:
+                pl.when(p != 2)(functools.partial(wait_halo, phase, buf, p))
+            else:
                 wait_halo(phase, buf, p)
 
+            add(p)
+            return carry
+
+        def add(p):
             x = lhs(p)
             for d in range(2):
                 part[d] += jnp.dot(x, adj[d, p], preferred_element_type=F32)
-            return carry
-
-        lax.fori_loop(0, sources - 1, step, 0)
-        last = fifth
+
+        add(0)
+        if forwards:
+            forward_halo(phase, buf)
+        order = (0, 1, 2, 4, 3) if forwards else (0, 1, 2, 3, 4)
+        last = order[-1]
+        lax.fori_loop(
+            0, 3, lambda i, carry: step(i + 1 + (i // 2) * (order[3] - 3), carry), 0
+        )
         wait_halo(phase, buf, last)
         x = lhs(last)
         part[other] += jnp.dot(x, adj[other, last], preferred_element_type=F32)
@@ -221,6 +241,10 @@
     logit_sum = aggregate(1, x2, lambda p: projected_of(p).astype(BF16), width, rx2)
     for _ in counter:
         pass
+    if direct:
+        for copy in counts:
+            copy.wait()
+        cnt[...] += jnp.sum(cnt_rx[...], axis=0)
     train_count = cnt[0:1, 0:1]
     projected = jnp.dot(w2t_ref[...], hid[...], preferred_element_type=F32)
     logits = (logit_sum + projected) / degree
@@ -257,35 +281,77 @@
             at += grad.shape[0]
     grads[at:, :] = jnp.zeros((grads.shape[0] - at, TILE), F32) + loss_local
 
-    base = 0
-    bases = []
-    for k, (axis, bit, rows, halved) in enumerate(plan):
-        peer = level_peer(axis, bit)
-        mine = level_bit(axis, bit)
-        bases.append(base)
-        if halved:
-            keep = pl.multiple_of(base + mine * rows, 8)
-            away = pl.multiple_of(base + (1 - mine) * rows, 8)
-        else:
-            keep = away = base
+    if direct:
+        half = grads.shape[0] // 2
+        rows = half // row_total
+        mine = pl.multiple_of(col * half, 8)
+        away = pl.multiple_of(other * half, 8)
         copy = remote(
-            grads.at[pl.ds(away, rows), :], grad_rx[k], sum_send.at[k], sum_recv.at[k], peer
+            grads.at[pl.ds(away, half), :], grad_rx[0], sum_send.at[0], sum_recv.at[0],
+            {"col": other},
         )
         copy.start()
         copy.wait()
-        grads[pl.ds(keep, rows), :] += grad_rx[k][...]
-        base = keep
-    rows = plan[-1][2]
-    gathered[pl.ds(base, rows), :] = grads[pl.ds(base, rows), :]
-    for k in range(len(plan) - 1, -1, -1):
-        axis, bit, rows, halved = plan[k]
-        if not halved:
-            continue
-        mine = level_bit(axis, bit)
-        piece = gathered.at[pl.ds(pl.multiple_of(bases[k] + mine * rows, 8), rows), :]
-        copy = remote(piece, piece, all_send.at[k], all_recv.at[k], level_peer(axis, bit))
+        grads[pl.ds(mine, half), :] += grad_rx[0][...]
+        hops = sorted(range(1, row_total), key=lambda by: -min(by, row_total - by))
+        piece = pl.multiple_of(mine + here * rows, 8)
+        copies = []
+        for by in hops:
+            there = lax.rem(here + by, row_total)
+            copies.append(remote(
+                grads.at[pl.ds(pl.multiple_of(mine + there * rows, 8), rows), :],
+                grad_rx[1].at[by - 1], sum_send.at[by], sum_recv.at[by], {"row": there},
+            ))
+            copies[-1].start()
+        for copy in copies:
+            copy.wait()
+        gathered[pl.ds(piece, rows), :] = grads[pl.ds(piece, rows), :] + jnp.sum(
+            grad_rx[1][...], axis=0
+        )
+        copies = []
+        for by in hops:
+            there = lax.rem(here + by, row_total)
+            spot = gathered.at[pl.ds(piece, rows), :]
+            copies.append(
+                remote(spot, spot, all_send.at[by], all_recv.at[by], {"row": there})
+            )
+            copies[-1].start()
+        for copy in copies:
+            copy.wait()
+        spot = gathered.at[pl.ds(mine, half), :]
+        copy = remote(spot, spot, all_send.at[0], all_recv.at[0], {"col": other})
         copy.start()
         copy.wait()
+    else:
+        base = 0
+        bases = []
+        for k, (axis, bit, rows, halved) in enumerate(plan):
+            peer = level_peer(axis, bit)
+            mine = level_bit(axis, bit)
+            bases.append(base)
+            if halved:
+                keep = pl.multiple_of(base + mine * rows, 8)
+                away = pl.multiple_of(base + (1 - mine) * rows, 8)
+            else:
+                keep = away = base
+            copy = remote(
+                grads.at[pl.ds(away, rows), :], grad_rx[k], sum_send.at[k], sum_recv.at[k], peer
+            )
+            copy.start()
+            copy.wait()
+            grads[pl.ds(keep, rows), :] += grad_rx[k][...]
+            base = keep
+        rows = plan[-1][2]
+        gathered[pl.ds(base, rows), :] = grads[pl.ds(base, rows), :]
+        for k in range(len(plan) - 1, -1, -1):
+            axis, bit, rows, halved = plan[k]
+            if not halved:
+                continue
+            mine = level_bit(axis, bit)
+            piece = gathered.at[pl.ds(pl.multiple_of(bases[k] + mine * rows, 8), rows), :]
+            copy = remote(piece, piece, all_send.at[k], all_recv.at[k], level_peer(axis, bit))
+            copy.start()
+            copy.wait()
     for start, count, out, lane in spots:
         out[:, lane:lane + TILE] = gathered[start:start + count, :]
     loss_out[...] = gathered[at:at + 8, :] / cnt[...]
@@ -324,7 +390,13 @@
     grad_rows = (f_in + width) * (hidden_total // TILE)
     grad_rows = ceil_to(grad_rows + 8, 128)
     plan = reduce_plan(grad_rows, row_total)
-    levels = len(plan)
+    direct = row_total <= 8
+    levels = 2 * row_total if direct else len(plan)
+    if direct:
+        half = grad_rows // 2
+        grad_buffers = [(half, TILE), (row_total - 1, half // row_total, TILE)]
+    else:
+        grad_buffers = [(rows, TILE) for _, _, rows, _ in plan]
     vmem = pl.BlockSpec(memory_space=pltpu.VMEM)
     dma = pltpu.SemaphoreType.DMA
     logits_t, grad_one, grad_two_t, loss = pl.pallas_call(
@@ -349,11 +421,11 @@
             pltpu.VMEM((width, nodes), F32),
             pltpu.VMEM((hidden_total, nodes), BF16),
             pltpu.VMEM((8, TILE), F32),
-            pltpu.VMEM((levels, 8, TILE), F32),
+            pltpu.VMEM((levels - 1 if direct else levels, 8, TILE), F32),
             pltpu.VMEM((grad_rows, TILE), F32),
             pltpu.VMEM((grad_rows, TILE), F32),
         ]
-        + [pltpu.VMEM((rows, TILE), F32) for _, _, rows, _ in plan]
+        + [pltpu.VMEM(shape, F32) for shape in grad_buffers]
         + [dma((3, sources, CHUNKS)), dma((3, sources, CHUNKS)), dma((3,)), dma((3,))]
         + [dma((levels,)) for _ in range(6)],
         compiler_params=pltpu.CompilerParams(

time: 131 us -> 112 us (0.85)
  Pallas kernels: 122 us -> 104 us
    pallas_call x1, Pallas kernels: 122 us -> 104 us  [shards(): pl.pallas_call(functools.partial(kernel, row_total, classes, plan), out_s...]
where the time goes in v3:
time: 112 us
  Pallas kernels  104 us (93%)
  local copies, waits for them, and re-layouts  6.8 us (6%)
  between operations  1.48 us (1%)
    pallas_call x1, Pallas kernels, shards(): pl.pallas_call(functools.partial(kernel, row_total, classes, plan), out_s...  104 us
    unnamed x23, local copies, waits for them, and re-layouts  4.64 us

profile of v3, /device:TPU:0, one launch (start us, length us, event | category | flops | bytes accessed | tf_op | source)
XLA Modules:
  0.0 112.0 jit_solution(16396468822673987370)
XLA Ops:
  0.6 0.0 copy-start.2
  1.4 0.0 copy-start.7
  1.4 0.0 copy-start.8
  1.4 0.6 copy-done.7
  2.0 0.0 copy-done.8
  2.1 0.0 copy-start.5
  2.1 0.1 select_reduce_fusion
  2.2 0.6 copy-done.5
  2.8 0.0 copy-start.6
  2.8 0.7 copy-done.6
  3.4 0.0 copy-done.2
  3.4 0.0 copy-start.3
  3.5 0.0 copy-start.4
  3.5 0.1 copy.19
  3.6 0.0 copy-start.1
  3.6 0.6 copy-done.3
  4.2 0.0 copy-done.4
  4.2 0.2 copy-done.1
  4.5 0.1 copy.20
  4.6 0.0 copy-start
  4.6 0.1 copy.21.w2t_ref
  4.7 0.8 copy-done
  5.6 0.1 copy.18
  5.7 103.6 %shard_map.129 = (f32[176,768]{1,0:T(8,128)S(1)}, f32[128,256]{1,0:T(8,128)S(1)}, f32[176,256]{1,0:T(8,128)S(1)}, f32[8,128]{1,0:T(8,128)S(1)}) custom-call(s32[360]{0:T(512)S(1)} %broadcast_add_fusion.map_ref, f32[128,768]{1,0:T(8,128)S(1)} %convert_bitcast_fusion.feat_ref, bf16[256,128]{1,0:T(8,128)(2,1)S(1)} %bitcast.37, ...), custom_call_target="tpu_custom_call" | custom-call | tf_op jit(solution)/shard_map/pallas_call | solution.py:402
  109.3 0.5 slice.10
  109.8 0.8 slice_bitcast_fusion
  110.7 0.7 slice_bitcast_fusion.1
  111.4 0.7 copy.28
  (7 shorter events, 0.1 us)
Async XLA Ops:
  0.6 2.8 %copy-start.2 = (bf16[128,256]{1,0:T(8,128)(2,1)S(1)}, bf16[128,256]{1,0:T(8,128)(2,1)}, u32[]{:S(2)}) copy-start(bf16[128,256]{1,0:T(8,128)(2,1)} %param.13) | copy-start | bytes 196612
  1.4 0.7 copy-start.7
  1.4 0.7 copy-start.8
  2.1 0.7 copy-start.5
  2.8 0.7 copy-start.6
  3.4 0.8 copy-start.3
  3.5 0.8 copy-start.4
  3.6 0.9 copy-start.1
  4.6 0.9 copy-start

commit v4 on v3

--- a/solution.py
+++ b/solution.py
@@ -169,6 +169,8 @@
 
     lax.fori_loop(0, slots, build, 0, unroll=2)
     tiles[slots] = jnp.zeros((TILE, TILE), BF16)
+    if forwards:
+        forward_halo(0, x1)
     next(counter, None)
 
     def place(p, carry):
@@ -201,7 +203,7 @@
                 part[d] += jnp.dot(x, adj[d, p], preferred_element_type=F32)
 
         add(0)
-        if forwards:
+        if forwards and phase > 0:
             forward_halo(phase, buf)
         order = (0, 1, 2, 4, 3) if forwards else (0, 1, 2, 3, 4)
         last = order[-1]
@@ -238,6 +240,7 @@
         return jnp.dot(w2t_ref[...], hidden_of(p), preferred_element_type=F32)
 
     hid[...] = hidden_of(0)
+    x3[0] = jnp.dot(w2t_ref[...], hid[...], preferred_element_type=F32)
     logit_sum = aggregate(1, x2, lambda p: projected_of(p).astype(BF16), width, rx2)
     for _ in counter:
         pass
@@ -246,8 +249,7 @@
             copy.wait()
         cnt[...] += jnp.sum(cnt_rx[...], axis=0)
     train_count = cnt[0:1, 0:1]
-    projected = jnp.dot(w2t_ref[...], hid[...], preferred_element_type=F32)
-    logits = (logit_sum + projected) / degree
+    logits = (logit_sum + x3[0]) / degree
     logits_out[...] = logits
     class_ids = lax.broadcasted_iota(jnp.int32, (width, nodes), 0)
     masked = jnp.where(class_ids < classes, logits, -jnp.inf)

time: 112 us -> 112 us (level)
  no operation moved by 1% of the time
where the time goes in v4:
time: 112 us
  Pallas kernels  104 us (93%)
  local copies, waits for them, and re-layouts  6.8 us (6%)
  between operations  1.48 us (1%)
    pallas_call x1, Pallas kernels, shards(): pl.pallas_call(functools.partial(kernel, row_total, classes, plan), out_s...  104 us
    unnamed x23, local copies, waits for them, and re-layouts  4.64 us

profile of v4, /device:TPU:0, one launch (start us, length us, event | category | flops | bytes accessed | tf_op | source)
XLA Modules:
  0.0 112.0 jit_solution(18306189968957655334)
XLA Ops:
  0.6 0.0 copy-start.2
  1.4 0.0 copy-start.7
  1.4 0.0 copy-start.8
  1.4 0.6 copy-done.7
  2.0 0.0 copy-done.8
  2.1 0.0 copy-start.5
  2.1 0.1 select_reduce_fusion
  2.2 0.6 copy-done.5
  2.8 0.0 copy-start.6
  2.8 0.7 copy-done.6
  3.4 0.0 copy-done.2
  3.4 0.0 copy-start.3
  3.5 0.0 copy-start.4
  3.5 0.1 copy.19
  3.6 0.0 copy-start.1
  3.6 0.6 copy-done.3
  4.2 0.0 copy-done.4
  4.2 0.2 copy-done.1
  4.5 0.1 copy.20
  4.6 0.0 copy-start
  4.6 0.1 copy.21.w2t_ref
  4.7 0.8 copy-done
  5.6 0.1 copy.18
  5.7 103.5 %shard_map.129 = (f32[176,768]{1,0:T(8,128)S(1)}, f32[128,256]{1,0:T(8,128)S(1)}, f32[176,256]{1,0:T(8,128)S(1)}, f32[8,128]{1,0:T(8,128)S(1)}) custom-call(s32[360]{0:T(512)S(1)} %broadcast_add_fusion.map_ref, f32[128,768]{1,0:T(8,128)S(1)} %convert_bitcast_fusion.feat_ref, bf16[256,128]{1,0:T(8,128)(2,1)S(1)} %bitcast.37, ...), custom_call_target="tpu_custom_call" | custom-call | tf_op jit(solution)/shard_map/pallas_call | solution.py:404
  109.3 0.5 slice.10
  109.8 0.8 slice_bitcast_fusion
  110.6 0.7 slice_bitcast_fusion.1
  111.3 0.7 copy.28
  (7 shorter events, 0.1 us)
Async XLA Ops:
  0.6 2.8 %copy-start.2 = (bf16[128,256]{1,0:T(8,128)(2,1)S(1)}, bf16[128,256]{1,0:T(8,128)(2,1)}, u32[]{:S(2)}) copy-start(bf16[128,256]{1,0:T(8,128)(2,1)} %param.13) | copy-start | bytes 196612
  1.4 0.7 copy-start.7
  1.4 0.7 copy-start.8
  2.1 0.7 copy-start.5
  2.8 0.7 copy-start.6
  3.4 0.8 copy-start.3
  3.5 0.8 copy-start.4
  3.6 0.9 copy-start.1
  4.6 0.9 copy-start
